TPU v7x, 32 devices: a whole 2x2x4 slice. The times are simulated.
32 devices in a mesh: dp: 2 (over core), seq: 16 (over z, y, x).
Axes of the slice: x: 2, y: 2, z: 4, core: 2. Of those that a mesh axis runs over, the one named last changes fastest.
Arguments:
- query: bfloat16 [2, 8192, 1536], P('dp', 'seq'), may hold values from -6 to 6
- key: bfloat16 [2, 8192, 1536], P('dp', 'seq'), may hold values from -6 to 6
- value: bfloat16 [2, 8192, 1536], P('dp', 'seq'), may hold values from -6 to 6
- block_weights: bfloat16 [64, 128, 128], P('seq', 'dp'), may hold values from -0.5 to 0.5
- mix_weights: bfloat16 [128, 64, 64], P('seq', 'dp'), may hold values from -1.5 to 1.5
- block_index: int32 [64, 16], replicated, may hold values from 0 to 63, all different within a row
- cotangent: bfloat16 [2, 8192, 1536], P('dp', 'seq'), may hold values from -6 to 6
Outputs:
- output: bfloat16 [2, 8192, 1536], P('dp', 'seq')
- grad_query: bfloat16 [2, 8192, 1536], P('dp', 'seq')
- grad_key: bfloat16 [2, 8192, 1536], P('dp', 'seq')
- grad_value: bfloat16 [2, 8192, 1536], P('dp', 'seq')
- grad_blocks: float32 [64, 128, 128], P('seq', 'dp')
- grad_mix: float32 [128, 64, 64], P('seq', 'dp')
Inputs may be any that keep to these rules, and one draw needn't show every extreme that they name: `block_index`: each row names 16 different blocks, and every block is named by some row.
All inputs are finite; a program needn't handle non-finite values.
Results may differ from a plain program's by a relative error of at most 0.0064.
Values may be sent and summed in bfloat16 or wider, within the bound.
A program may use at most 64 MiB of HBM per device.

v0:
```python
import jax
import jax.numpy as jnp
from jax import lax
from jax.sharding import PartitionSpec as P


def on_device(query, key, value, block_weights, mix_weights, block_index, cotangent):
    block_count = block_index.shape[0]
    block_size = block_weights.shape[2]
    samples, positions, channels = query.shape
    local_blocks = positions // block_size
    full_blocks = lax.all_gather(block_weights, "dp", axis=1, tiled=True)
    full_mix = lax.all_gather(mix_weights, "dp", axis=1, tiled=True)
    columns_all = jnp.arange(block_count, dtype=jnp.int32)
    pattern = jnp.max(
        (block_index[:, :, None] == columns_all[None, None, :]).astype(jnp.float32), axis=1
    )
    masked = (full_mix.astype(jnp.float32) * pattern[None]).astype(jnp.bfloat16)
    query_f = query.astype(jnp.float32)
    cot_f = cotangent.astype(jnp.float32)
    product = (key.astype(jnp.float32) * value.astype(jnp.float32)).astype(jnp.bfloat16)
    split_parts = product.reshape(samples, local_blocks, block_size, channels)
    first_factor = jnp.einsum(
        "iac,nicd->niad", full_blocks, split_parts, preferred_element_type=jnp.float32
    ).astype(jnp.bfloat16)
    grad_mixed = (
        (cot_f * query_f).astype(jnp.bfloat16).reshape(samples, local_blocks, block_size, channels)
    )

    def second(columns):
        return jnp.einsum(
            "jik,nkjd->nijd", masked, columns, preferred_element_type=jnp.float32
        ).astype(jnp.bfloat16)

    across, mixed_cols = (lambda columns: (columns, second(columns)))(
        lax.all_to_all(first_factor, "seq", split_axis=2, concat_axis=1, tiled=True)
    )
    returned = lax.all_to_all(mixed_cols, "seq", split_axis=1, concat_axis=2, tiled=True)
    grad_cols = lax.all_to_all(grad_mixed, "seq", split_axis=2, concat_axis=1, tiled=True)
    grad_first_cols = jnp.einsum(
        "jik,nijd->nkjd", masked, grad_cols, preferred_element_type=jnp.float32
    ).astype(jnp.bfloat16)
    first_factor_gradient = lax.all_to_all(
        grad_first_cols, "seq", split_axis=1, concat_axis=2, tiled=True
    )
    mix_terms = (
        jnp.einsum("nijd,nkjd->jik", grad_cols, across, preferred_element_type=jnp.float32)
        * pattern[None]
    )
    mixed_f = returned.reshape(samples, positions, channels).astype(jnp.float32)
    output = (query_f * mixed_f).astype(jnp.bfloat16)
    grad_query = (cot_f * mixed_f).astype(jnp.bfloat16)
    product_gradient = jnp.einsum(
        "iac,niad->nicd", full_blocks, first_factor_gradient, preferred_element_type=jnp.float32
    ).reshape(samples, positions, channels)
    grad_key = (product_gradient * value.astype(jnp.float32)).astype(jnp.bfloat16)
    grad_value = (product_gradient * key.astype(jnp.float32)).astype(jnp.bfloat16)
    block_terms = jnp.einsum(
        "niad,nicd->iac", first_factor_gradient, split_parts, preferred_element_type=jnp.float32
    )
    grad_mix = lax.psum_scatter(mix_terms, "dp", scatter_dimension=1, tiled=True)
    grad_blocks = lax.psum_scatter(block_terms, "dp", scatter_dimension=1, tiled=True)
    return (output, grad_query, grad_key, grad_value, grad_blocks, grad_mix)


def solution(mesh):
    placed = (
        P("dp", "seq", None),
        P("dp", "seq", None),
        P("dp", "seq", None),
        P("seq", "dp", None),
        P("seq", "dp", None),
        P(),
        P("dp", "seq", None),
    )
    return jax.shard_map(
        on_device,
        mesh=mesh,
        in_specs=placed,
        out_specs=(
            P("dp", "seq", None),
            P("dp", "seq", None),
            P("dp", "seq", None),
            P("dp", "seq", None),
            P("seq", "dp", None),
            P("seq", "dp", None),
        ),
        check_vma=False,
    )
```

profile of v0, /device:TPU:0, one launch (start us, length us, event | category | flops | bytes accessed | tf_op | source)
XLA Modules:
  0.0 211.0 jit_solution(2744378990846585952)
XLA Ops:
  7.2 2.3 %fusion.5 = bf16[1,512,1536]{2,1,0:T(8,128)(2,1)S(1)} fusion(bf16[1,512,1536]{2,1,0:T(8,128)(2,1)} %param.7, bf16[1,512,1536]{2,1,0:T(8,128)(2,1)} %param.13), kind=kLoop, calls=%fused_computation.11 | loop fusion | flops 3145728 | bytes 4718592 | tf_op jit(solution)/shard_map/convert_element_type | solution.py:27
  9.4 2.4 %copy.59 = bf16[1,4,128,1536]{3,1,0,2:T(4,128)(2,1)} copy(bf16[1,4,128,1536]{3,2,1,0:T(8,128)(2,1)S(1)} %bitcast.62) | data formatting | bytes 3145728 | tf_op jit(solution)/shard_map/reshape | solution.py:27
  11.8 0.0 copy-start.8
  11.8 0.0 copy-start.6
  11.8 8.4 %all-to-all-start.2 = ((bf16[1,4,128,1536]{3,1,0,2:T(4,128)(2,1)}), bf16[1,4,128,1536]{3,1,0,2:T(4,128)(2,1)S(1)}, u32[]{:S(2)}, u32[]{:S(2)}) async-start(bf16[1,4,128,1536]{3,1,0,2:T(4,128)(2,1)} %copy.59), calls=%async_computation.2 | async-start | bytes 3145728 | tf_op jit(solution)/shard_map/all_to_all | solution.py:39
  20.2 0.0 copy-done.8
  20.3 0.1 copy.56
  20.3 0.0 copy-done.6
  20.3 1.9 all_gather.7
  22.2 0.2 convert_reduce_fusion
  22.5 31.9 %all-to-all-done.2 = bf16[1,4,128,1536]{3,1,0,2:T(4,128)(2,1)S(1)} async-done(((bf16[1,4,128,1536]{3,1,0,2:T(4,128)(2,1)}), bf16[1,4,128,1536]{3,1,0,2:T(4,128)(2,1)S(1)}, u32[]{:S(2)}, u32[]{:S(2)}) %all-to-all-start.2) | async-done | bytes 1572896 | tf_op jit(solution)/shard_map/all_to_all | solution.py:39
  54.4 0.3 copy.77
  54.7 1.2 copy.61
  55.9 0.4 reshape.73
  56.3 0.6 fusion.7
  56.9 2.0 copy.63
  59.0 0.0 copy-start.7
  59.0 7.8 %all-to-all-start.3 = ((bf16[1,64,8,1536]{3,2,0,1:T(8,128)(2,1)}), bf16[1,64,8,1536]{3,2,0,1:T(8,128)(2,1)S(1)}, u32[]{:S(2)}, u32[]{:S(2)}) async-start(bf16[1,64,8,1536]{3,2,0,1:T(8,128)(2,1)} %copy.63), calls=%async_computation.3 | async-start | bytes 3145728 | tf_op jit(solution)/shard_map/all_to_all | solution.py:43
  66.7 0.0 copy-done.7
  66.7 1.9 all_gather.6
  68.6 31.6 %all-to-all-done.3 = bf16[1,64,8,1536]{3,2,0,1:T(8,128)(2,1)S(1)} async-done(((bf16[1,64,8,1536]{3,2,0,1:T(8,128)(2,1)}), bf16[1,64,8,1536]{3,2,0,1:T(8,128)(2,1)S(1)}, u32[]{:S(2)}, u32[]{:S(2)}) %all-to-all-start.3) | async-done | bytes 1572896 | tf_op jit(solution)/shard_map/all_to_all | solution.py:43
  100.2 0.0 copy-start.2
  100.2 0.6 fusion.11
  100.9 0.5 copy-done.2
  101.4 0.8 copy-done.4
  102.2 0.5 copy-done.5
  102.7 2.6 %fusion.1 = (bf16[1,512,1536]{2,1,0:T(8,128)(2,1)}, bf16[1,512,1536]{2,1,0:T(8,128)(2,1)}, bf16[1,512,1536]{2,1,0:T(8,128)(2,1)S(1)}) fusion(bf16[1,512,1536]{2,1,0:T(8,128)(2,1)S(1)} %copy-done.4, f32[4,1536,128]{1,2,0:T(8,128)S(1)} %fusion.11, bf16[1,512,1536]{2,1,0:T(8,128)(2,1)S(1)} %copy-done.5), kind=kLoop, calls=%fused_computation.7 | loop fusion | flops 6291456 | bytes 11010048 | tf_op jit(solution)/shard_map/convert_element_type | solution.py:57
  105.3 1.1 copy-done.3
  106.4 0.7 fusion.6
  107.2 2.5 %copy.53 = bf16[1,4,128,1536]{3,1,0,2:T(4,128)(2,1)} copy(bf16[1,4,128,1536]{2,3,1,0:T(8,128)(2,1)S(1)} %fusion.6) | data formatting | bytes 3145728 | tf_op jit(solution)/shard_map/convert_element_type | solution.py:25
  109.6 44.2 %all_to_all.54 = bf16[1,4,128,1536]{3,1,0,2:T(4,128)(2,1)S(1)} all-to-all(bf16[1,4,128,1536]{3,1,0,2:T(4,128)(2,1)} %copy.53), channel_id=1, replica_groups=mesh['dp'=2,'seq'=16] {'seq'}, dimensions={2} | all-to-all | bytes 3145728 | tf_op jit(solution)/shard_map/all_to_all | solution.py:36
  153.8 0.3 copy.78
  154.1 2.4 %copy.55 = bf16[1,16,4,8,1536]{4,2,1,3,0:T(4,128)(2,1)} copy(bf16[1,16,4,8,1536]{4,3,1,2,0:T(8,128)(2,1)S(1)} %bitcast.59) | data formatting | bytes 3145728 | tf_op jit(solution)/shard_map/all_to_all | solution.py:36
  156.5 2.7 %reshape.71 = bf16[64,8,1536]{2,0,1:T(8,128)(2,1)S(1)} reshape(bf16[1,16,4,8,1536]{4,2,1,3,0:T(4,128)(2,1)} %copy.55) | data formatting | bytes 3145728 | tf_op jit(solution)/shard_map/reshape.2
  159.2 0.5 fusion.8
  159.8 2.0 copy.57
  161.8 4.4 %all-to-all-start.1 = ((bf16[1,64,8,1536]{3,2,0,1:T(8,128)(2,1)}), bf16[1,64,8,1536]{3,2,0,1:T(8,128)(2,1)}, u32[]{:S(2)}, u32[]{:S(2)}) async-start(bf16[1,64,8,1536]{3,2,0,1:T(8,128)(2,1)} %copy.57), calls=%async_computation.1 | async-start | bytes 3145728 | tf_op jit(solution)/shard_map/all_to_all | solution.py:38
  166.2 0.0 reduce-scatter.3.cloned.1.call-start
  166.2 3.1 %fusion.9 = f32[4,128,128]{2,1,0:T(8,128)} fusion(bf16[4,128,1536]{2,1,0:T(8,128)(2,1)} %bitcast.64, bf16[1,16,4,8,1536]{4,3,2,1,0:T(8,128)(2,1)} %bitcast.61), kind=kOutput, calls=%fused_computation.18 | convolution fusion | flops 201326592 | bytes 3407872 | tf_op jit(solution)/shard_map/niad,nicd->iac/dot_general | solution.py:58
  169.4 0.0 reduce-scatter.3.cloned.1.call-update
  169.4 0.0 reduce-scatter.5.cloned.1.call-start
  169.5 1.3 convolution_multiply_fusion
  170.7 0.0 reduce-scatter.5.cloned.1.call-update
  170.7 28.5 %all-to-all-done.1 = bf16[1,64,8,1536]{3,2,0,1:T(8,128)(2,1)} async-done(((bf16[1,64,8,1536]{3,2,0,1:T(8,128)(2,1)}), bf16[1,64,8,1536]{3,2,0,1:T(8,128)(2,1)}, u32[]{:S(2)}, u32[]{:S(2)}) %all-to-all-start.1) | async-done | bytes 1572896 | tf_op jit(solution)/shard_map/all_to_all | solution.py:38
  199.3 1.9 copy.58
  201.3 0.0 copy-done
  201.3 0.4 copy-done.1
  201.7 2.5 %fusion.4 = (bf16[1,512,1536]{2,1,0:T(8,128)(2,1)}, bf16[1,512,1536]{2,1,0:T(8,128)(2,1)}) fusion(bf16[1,512,1536]{2,1,0:T(8,128)(2,1)S(1)} %copy-done, f32[1,16,4,8,1536]{4,3,1,2,0:T(8,128)S(1)} %copy.58, bf16[1,512,1536]{2,1,0:T(8,128)(2,1)S(1)} %copy-done.1), kind=kLoop, calls=%fused_computation.10 | loop fusion | flops 4718592 | bytes 9437184 | tf_op jit(solution)/shard_map/convert_element_type | solution.py:52
  (7 shorter events, 0.0 us)
Async XLA Ops:
  11.8 8.5 %copy-start.8 = (s32[64,16]{0,1:T(8,128)S(1)}, s32[64,16]{0,1:T(8,128)}, u32[]{:S(2)}) copy-start(s32[64,16]{0,1:T(8,128)} %param.12) | copy-start | bytes 12292
  11.8 8.6 %copy-start.6 = (bf16[8,32,64]{2,1,0:T(8,128)(2,1)S(1)}, bf16[8,32,64]{2,1,0:T(8,128)(2,1)}, u32[]{:S(2)}) copy-start(bf16[8,32,64]{2,1,0:T(8,128)(2,1)} %param.11) | copy-start | bytes 98308
  11.8 42.6 %all-to-all-start.2 = ((bf16[1,4,128,1536]{3,1,0,2:T(4,128)(2,1)}), bf16[1,4,128,1536]{3,1,0,2:T(4,128)(2,1)S(1)}, u32[]{:S(2)}, u32[]{:S(2)}) async-start(bf16[1,4,128,1536]{3,1,0,2:T(4,128)(2,1)} %copy.59), calls=%async_computation.2 | async-start | bytes 3145728 | tf_op jit(solution)/shard_map/all_to_all | solution.py:39
  59.0 7.8 %copy-start.7 = (bf16[4,64,128]{2,1,0:T(8,128)(2,1)S(1)}, bf16[4,64,128]{2,1,0:T(8,128)(2,1)}, u32[]{:S(2)}) copy-start(bf16[4,64,128]{2,1,0:T(8,128)(2,1)} %param.10) | copy-start | bytes 196612
  59.0 41.3 %all-to-all-start.3 = ((bf16[1,64,8,1536]{3,2,0,1:T(8,128)(2,1)}), bf16[1,64,8,1536]{3,2,0,1:T(8,128)(2,1)S(1)}, u32[]{:S(2)}, u32[]{:S(2)}) async-start(bf16[1,64,8,1536]{3,2,0,1:T(8,128)(2,1)} %copy.63), calls=%async_computation.3 | async-start | bytes 3145728 | tf_op jit(solution)/shard_map/all_to_all | solution.py:43
  100.2 1.1 copy-start.2
  100.2 2.0 copy-start.4
  100.2 2.4 %copy-start.5 = (bf16[1,512,1536]{2,1,0:T(8,128)(2,1)S(1)}, bf16[1,512,1536]{2,1,0:T(8,128)(2,1)}, u32[]{:S(2)}) copy-start(bf16[1,512,1536]{2,1,0:T(8,128)(2,1)} %param.9) | copy-start | bytes 4718596
  105.3 1.1 copy-start.3
  161.8 37.5 %all-to-all-start.1 = ((bf16[1,64,8,1536]{3,2,0,1:T(8,128)(2,1)}), bf16[1,64,8,1536]{3,2,0,1:T(8,128)(2,1)}, u32[]{:S(2)}, u32[]{:S(2)}) async-start(bf16[1,64,8,1536]{3,2,0,1:T(8,128)(2,1)} %copy.57), calls=%async_computation.1 | async-start | bytes 3145728 | tf_op jit(solution)/shard_map/all_to_all | solution.py:38
  166.2 38.0 %reduce-scatter.3.cloned.1.call-start = ((), (), s32[]{:S(2)}) async-start(), calls=%async_computation.6 | async-start | bytes 393216 | tf_op jit(solution)/shard_map/reduce_scatter | solution.py:62
  169.4 34.7 %reduce-scatter.5.cloned.1.call-start = ((), (), s32[]{:S(2)}) async-start(), calls=%async_computation.7 | async-start | bytes 393216 | tf_op jit(solution)/shard_map/reduce_scatter | solution.py:61
  199.3 2.0 copy-start
  199.3 2.4 %copy-start.1 = (bf16[1,512,1536]{2,1,0:T(8,128)(2,1)S(1)}, bf16[1,512,1536]{2,1,0:T(8,128)(2,1)}, u32[]{:S(2)}) copy-start(bf16[1,512,1536]{2,1,0:T(8,128)(2,1)} %param.7) | copy-start | bytes 4718596
Sparse Core Ops, SparseCore 0:
  169.8 8.8 reduce-scatter.2
  181.6 8.8 reduce-scatter.4
where the time goes:
time: 213 us; the launch traced here: 211 us
  waiting for transfers between devices  92.1 us (43%)
  blocking collectives  48 us (23%)
  local copies, waits for them, and re-layouts  21.5 us (10%)
  starting transfers between devices  20.7 us (10%)
  between operations  14.2 us (7%)
  other arithmetic  7.59 us (4%)
  matrix products  6.91 us (3%)
    all_to_all x1, blocking collectives, on_device(): lax.all_to_all(first_factor, 'seq', split_axis=2, concat_axis=1, tiled=True)  44.2 us
    all_to_all x1, waiting for transfers between devices, on_device(): lax.all_to_all(grad_mixed, 'seq', split_axis=2, concat_axis=1, tiled=True)  31.9 us
    all_to_all x1, waiting for transfers between devices, on_device(): lax.all_to_all(grad_first_cols, 'seq', split_axis=1, concat_axis=2, tiled...  31.6 us
    all_to_all x1, waiting for transfers between devices, on_device(): lax.all_to_all(mixed_cols, 'seq', split_axis=1, concat_axis=2, tiled=True)  28.5 us
    all_to_all x1, starting transfers between devices, on_device(): lax.all_to_all(grad_mixed, 'seq', split_axis=2, concat_axis=1, tiled=True)  8.44 us
    all_to_all x1, starting transfers between devices, on_device(): lax.all_to_all(grad_first_cols, 'seq', split_axis=1, concat_axis=2, tiled...  7.77 us
    all_to_all x1, starting transfers between devices, on_device(): lax.all_to_all(mixed_cols, 'seq', split_axis=1, concat_axis=2, tiled=True)  4.4 us
  transfers between devices with their start and end apart: 5, of which 3 were waited for; matrix products, arithmetic and copies ran while one was open for 4% of the time, Pallas kernels for 0%

commit v1 on v0

v1 whole, which is shorter than its diff:
```python
import functools

import jax
import jax.numpy as jnp
from jax import lax
from jax.experimental import pallas as pl
from jax.experimental.pallas import tpu as pltpu
from jax.sharding import PartitionSpec as P

F32 = jnp.float32
BF16 = jnp.bfloat16
G, F, H, M = range(4)


def log2(x):
    return x.bit_length() - 1


def iota(shape, dim):
    return lax.broadcasted_iota(jnp.int32, shape, dim)


def onehot(cond):
    return jnp.where(cond, 1.0, 0.0).astype(BF16)


def dot(a, b):
    return jnp.dot(a, b, preferred_element_type=F32)


def dot_nt(a, b):
    return lax.dot_general(a, b, (((1,), (1,)), ((), ())), preferred_element_type=F32)


def dot_tn(a, b):
    return lax.dot_general(a, b, (((0,), (0,)), ((), ())), preferred_element_type=F32)


def thirds(x):
    hi = x.astype(BF16)
    rest = x - hi.astype(F32)
    mid = rest.astype(BF16)
    return hi, mid, (rest - mid.astype(F32)).astype(BF16)


def kernel(
    n, ndp, tile,
    q_ref, k_ref, v_ref, c_ref, w_ref, mx_ref, bi_ref,
    o_ref, gq_ref, gk_ref, gv_ref, gb_ref, gm_ref,
    gs, gr, fs, fr, hs, hr, ms, mr,
    prod, gfn, bmat, btm, wfull, wg, mg, pr, gms, gmr, gbs, gbr,
    send, recv, dsend, drecv, lsem, wsem,
):
    rows, width = q_ref.shape
    blocks, bs = w_ref.shape[0], w_ref.shape[2]
    nb, nnz = bi_ref.shape
    offs = bs // n
    chunk = blocks * offs
    own = nb // ndp
    part = own * offs
    a_loc = w_ref.shape[1]
    me = lax.axis_index("seq")
    core = lax.axis_index("dp")

    def peer(i):
        return lax.rem(me + 1 + lax.rem(n // 2 - 1 + 4 * i, n - 1), n)

    def mate(i):
        return lax.rem(core + 1 + i, ndp)

    barrier = pltpu.get_barrier_semaphore()

    @pl.loop(0, n - 1)
    def _(i):
        pl.semaphore_signal(
            barrier, inc=1, device_id={"dp": core, "seq": lax.rem(me + 1 + i, n)},
            device_id_type=pl.DeviceIdType.MESH,
        )

    @pl.loop(0, ndp - 1)
    def _(i):
        pl.semaphore_signal(
            barrier, inc=1, device_id={"dp": mate(i), "seq": me},
            device_id_type=pl.DeviceIdType.MESH,
        )

    pl.semaphore_wait(barrier, n + ndp - 2)

    def across(kind, src, dst, to, slot):
        return pltpu.make_async_remote_copy(
            src_ref=src.at[to], dst_ref=dst.at[slot],
            send_sem=send.at[kind, to], recv_sem=recv.at[kind, slot],
            device_id={"dp": core, "seq": to}, device_id_type=pl.DeviceIdType.MESH,
        )

    def exchange(kind, src, dst):
        @pl.loop(0, n - 1)
        def _(i):
            across(kind, src, dst, peer(i), me).start()

        pltpu.make_async_copy(src.at[me], dst.at[me], lsem.at[kind]).start()

    def arrived(kind, src, dst):
        @pl.loop(0, n - 1)
        def _(i):
            across(kind, src, dst, me, peer(i)).wait_recv()

        pltpu.make_async_copy(src.at[me], dst.at[me], lsem.at[kind]).wait()

    def left(kind, src, dst):
        @pl.loop(0, n - 1)
        def _(i):
            across(kind, src, dst, peer(i), me).wait_send()

    def beside(kind, src, dst, to, slot):
        return pltpu.make_async_remote_copy(
            src_ref=src, dst_ref=dst.at[slot],
            send_sem=dsend.at[kind, to], recv_sem=drecv.at[kind, slot],
            device_id={"dp": to, "seq": me}, device_id_type=pl.DeviceIdType.MESH,
        )

    def columns(body):
        @pl.loop(0, width // tile)
        def _(t):
            body(pl.ds(pl.multiple_of(t * tile, tile), tile))

    def place(shape, row_dim):
        r = iota(shape, row_dim)
        rem = r & (chunk - 1)
        return (rem >> log2(offs)) * bs + (r >> log2(chunk)) * offs + (rem & (offs - 1))

    def to_chunks(parts, dst, cols):
        if offs % 8 == 0:
            for p in range(n):
                span = slice(p * offs, (p + 1) * offs)
                dst[p, :, cols] = jnp.concatenate([x[span] for x in parts], axis=0).astype(BF16)
        else:
            order = onehot(place((rows, rows), 0) == iota((rows, rows), 1))
            whole = jnp.concatenate(parts, axis=0).astype(BF16)
            dst[:, :, cols] = dot(order, whole).astype(BF16).reshape(n, chunk, tile)

    def from_chunks(src, cols):
        if offs % 8 == 0:
            pieces = [src[p, :, cols].astype(F32) for p in range(n)]
            return [
                jnp.concatenate([x[b * offs : (b + 1) * offs] for x in pieces], axis=0)
                for b in range(blocks)
            ]
        order = onehot(place((rows, rows), 1) == iota((rows, rows), 0))
        whole = dot(order, src[:, :, cols].reshape(rows, tile))
        return [whole[b * bs : (b + 1) * bs] for b in range(blocks)]

    @pl.loop(0, ndp - 1)
    def _(i):
        beside(0, w_ref, wg, mate(i), core).start()
        beside(1, mx_ref, mg, mate(i), core).start()

    def gate(cols):
        parts = []
        for b in range(blocks):
            span = slice(b * bs, (b + 1) * bs)
            parts.append(c_ref[span, cols].astype(F32) * q_ref[span, cols].astype(F32))
        to_chunks(parts, gs, cols)

    columns(gate)
    exchange(G, gs, gr)

    wg[core] = w_ref[...]
    mg[core] = mx_ref[...]

    @pl.loop(0, ndp - 1)
    def _(i):
        beside(0, w_ref, wg, core, mate(i)).wait_recv()
        beside(1, mx_ref, mg, core, mate(i)).wait_recv()

    for h in range(ndp):
        wfull[:, h * a_loc : (h + 1) * a_loc, :] = wg[h]

    def first(cols):
        parts = []
        for b in range(blocks):
            span = slice(b * bs, (b + 1) * bs)
            x = (k_ref[span, cols].astype(F32) * v_ref[span, cols].astype(F32)).astype(BF16)
            prod[span, cols] = x
            parts.append(dot(wfull[b], x))
        to_chunks(parts, fs, cols)

    columns(first)
    exchange(F, fs, fr)

    named = jnp.zeros((nb, nb), F32)
    index = bi_ref[...]
    for t in range(nnz):
        named = jnp.where(index[:, t : t + 1] == iota((nb, nb), 1), 1.0, named)
    named = named.astype(BF16)
    spread = onehot((iota((nb, rows), 1) >> log2(offs)) == iota((nb, rows), 0))
    same = ((iota((part, rows), 0) ^ iota((part, rows), 1)) & (offs - 1)) == 0
    r, c = iota((part, part), 0), iota((part, part), 1)
    by_block = onehot((r & (offs - 1)) * own + (r >> log2(offs)) == c)
    by_offset = onehot((c & (offs - 1)) * own + (c >> log2(offs)) == r)
    for h in range(ndp):
        span = slice(h * part, (h + 1) * part)
        lift = onehot((iota((part, nb), 0) >> log2(offs)) + h * own == iota((part, nb), 1))
        pattern = dot(lift, named)
        pr[h] = pattern
        masked = (dot(by_block, mg[h]) * pattern).astype(BF16)
        bmat[span, :] = jnp.where(same, dot(masked, spread), 0.0).astype(BF16)
    btm[...] = bmat[...].T

    def flat(ref, cols):
        return ref[:, :, cols].reshape(rows, tile)

    arrived(G, gs, gr)

    def grad_first(cols):
        hs[:, :, cols] = dot(btm[...], flat(gr, cols)).astype(BF16).reshape(n, chunk, tile)

    columns(grad_first)
    exchange(H, hs, hr)
    arrived(F, fs, fr)

    def mixed(cols):
        ms[:, :, cols] = dot(bmat[...], flat(fr, cols)).astype(BF16).reshape(n, chunk, tile)

    columns(mixed)
    exchange(M, ms, mr)

    step = part // chunk
    for h in range(ndp):
        lhs = gr[h * step : (h + 1) * step].reshape(part, width)
        terms = jnp.where(same, dot_nt(lhs, fr[...].reshape(rows, width)), 0.0)
        kept = sum(dot_nt(x, spread) for x in thirds(terms))
        gms[h] = kept * pr[h]

    @pl.loop(0, ndp - 1)
    def _(i):
        beside(2, gms.at[mate(i)], gmr, mate(i), core).start()

    arrived(H, hs, hr)

    def grad_inputs(cols):
        parts = from_chunks(hr, cols)
        for b in range(blocks):
            span = slice(b * bs, (b + 1) * bs)
            x = parts[b].astype(BF16)
            gfn[span, cols] = x
            gp = dot_tn(wfull[b], x)
            gk_ref[span, cols] = (gp * v_ref[span, cols].astype(F32)).astype(BF16)
            gv_ref[span, cols] = (gp * k_ref[span, cols].astype(F32)).astype(BF16)

    columns(grad_inputs)
    for b in range(blocks):
        span = slice(b * bs, (b + 1) * bs)
        terms = dot_nt(gfn[span, :], prod[span, :])
        for h in range(ndp):
            gbs[h, b] = terms[h * a_loc : (h + 1) * a_loc]

    @pl.loop(0, ndp - 1)
    def _(i):
        beside(3, gbs.at[mate(i)], gbr, mate(i), core).start()

    gmr[core] = gms[core]
    gbr[core] = gbs[core]

    @pl.loop(0, ndp - 1)
    def _(i):
        beside(2, gms.at[mate(i)], gmr, core, mate(i)).wait_recv()
        beside(3, gbs.at[mate(i)], gbr, core, mate(i)).wait_recv()

    gb_ref[...] = sum(gbr[h] for h in range(ndp))
    total = sum(gmr[h] for h in range(ndp))
    gm_ref[...] = sum(dot(by_offset, x) for x in thirds(total))

    @pl.loop(0, ndp - 1)
    def _(i):
        beside(0, w_ref, wg, mate(i), core).wait_send()
        beside(1, mx_ref, mg, mate(i), core).wait_send()
        beside(2, gms.at[mate(i)], gmr, mate(i), core).wait_send()
        beside(3, gbs.at[mate(i)], gbr, mate(i), core).wait_send()

    left(G, gs, gr)
    left(F, fs, fr)
    left(H, hs, hr)
    arrived(M, ms, mr)

    def outputs(cols):
        parts = from_chunks(mr, cols)
        for b in range(blocks):
            span = slice(b * bs, (b + 1) * bs)
            o_ref[span, cols] = (q_ref[span, cols].astype(F32) * parts[b]).astype(BF16)
            gq_ref[span, cols] = (c_ref[span, cols].astype(F32) * parts[b]).astype(BF16)

    columns(outputs)
    left(M, ms, mr)


def on_device(n, ndp, query, key, value, block_weights, mix_weights, block_index, cotangent):
    _, rows, width = query.shape
    nb = block_index.shape[0]
    blocks, a_loc, bs = block_weights.shape
    offs, own, _ = mix_weights.shape
    chunk, part = blocks * offs, own * offs
    wide = jax.ShapeDtypeStruct((rows, width), BF16)
    vmem = pl.BlockSpec(memory_space=pltpu.VMEM)
    moved = pltpu.VMEM((n, chunk, width), BF16)
    dma = pltpu.SemaphoreType.DMA
    outs = pl.pallas_call(
        functools.partial(kernel, n, ndp, 256),
        out_shape=(
            wide, wide, wide, wide,
            jax.ShapeDtypeStruct((blocks, a_loc, bs), F32),
            jax.ShapeDtypeStruct((offs * own, nb), F32),
        ),
        in_specs=[vmem] * 7,
        out_specs=(vmem,) * 6,
        scratch_shapes=[moved] * 8 + [
            pltpu.VMEM((rows, width), BF16),
            pltpu.VMEM((rows, width), BF16),
            pltpu.VMEM((rows, rows), BF16),
            pltpu.VMEM((rows, rows), BF16),
            pltpu.VMEM((blocks, bs, bs), BF16),
            pltpu.VMEM((ndp, blocks, a_loc, bs), BF16),
            pltpu.VMEM((ndp, offs * own, nb), BF16),
            pltpu.VMEM((ndp, part, nb), F32),
            pltpu.VMEM((ndp, part, nb), F32),
            pltpu.VMEM((ndp, part, nb), F32),
            pltpu.VMEM((ndp, blocks, a_loc, bs), F32),
            pltpu.VMEM((ndp, blocks, a_loc, bs), F32),
            dma((4, n)), dma((4, n)), dma((4, ndp)), dma((4, ndp)), dma((4,)), dma((8,)),
        ],
        compiler_params=pltpu.CompilerParams(
            collective_id=0, has_side_effects=True, vmem_limit_bytes=56 * 1024 * 1024
        ),
        cost_estimate=pl.CostEstimate(
            flops=7 * 2 * rows * rows * width, bytes_accessed=16 * rows * width, transcendentals=0
        ),
        name="monarch",
    )(
        query[0], key[0], value[0], cotangent[0],
        block_weights, mix_weights.reshape(offs * own, nb), block_index,
    )
    output, grad_query, grad_key, grad_value, grad_blocks, grad_mix = outs
    return (
        output[None], grad_query[None], grad_key[None], grad_value[None],
        grad_blocks, grad_mix.reshape(offs, own, nb),
    )


def solution(mesh):
    wide, split = P("dp", "seq", None), P("seq", "dp", None)
    return jax.shard_map(
        functools.partial(on_device, mesh.shape["seq"], mesh.shape["dp"]),
        mesh=mesh,
        in_specs=(wide, wide, wide, split, split, P(), wide),
        out_specs=(wide, wide, wide, wide, split, split),
        check_vma=False,
    )
```

time: 213 us -> 161 us (0.76)
  Pallas kernels: 0 us -> 150 us
  waiting for transfers between devices: 92.1 us -> 0 us
  blocking collectives: 48 us -> 0 us
  starting transfers between devices: 20.7 us -> 0 us
  between operations: 14.2 us -> 0.66 us
  local copies, waits for them, and re-layouts: 21.5 us -> 10.6 us
  other arithmetic: 7.59 us -> 0 us
  matrix products: 6.91 us -> 0 us
    pallas_call x0 -> x1, Pallas kernels: none -> 150 us  [on_device(): pl.pallas_call(functools.partial(kernel, n, ndp, 256), out_shape=(wide, w...]
    all_to_all x3 -> x0, waiting for transfers between devices: 92.1 us -> none  [the longest x1 31.9 us: on_device(): lax.all_to_all(grad_mixed, 'seq', split_axis=2, concat_axis=1, tiled=True)]
    all_to_all x1 -> x0, blocking collectives: 44.2 us -> none  [on_device(): lax.all_to_all(first_factor, 'seq', split_axis=2, concat_axis=1, tiled=True)]
    all_to_all x3 -> x0, starting transfers between devices: 20.6 us -> none  [the longest x1 8.44 us: on_device(): lax.all_to_all(grad_mixed, 'seq', split_axis=2, concat_axis=1, tiled=True)]
    convert_element_type x4 -> x0, local copies, waits for them, and re-layouts: 8.43 us -> none  [the longest x1 2.46 us: on_device(): first_factor = jnp.einsum('iac,nicd->niad', full_blocks, split_parts, pre...]
    convert_element_type x3 -> x0, other arithmetic: 7.36 us -> none  [the longest x1 2.61 us: on_device(): (product_gradient * key.astype(jnp.float32)).astype(jnp.bfloat16)]
    unnamed x19 -> x17, local copies, waits for them, and re-layouts: 3.46 us -> 10.6 us
    dot_general x6 -> x0, matrix products: 6.91 us -> none  [the longest x1 3.15 us: on_device(): jnp.einsum('niad,nicd->iac', first_factor_gradient, split_parts, preferre...]
  transfers between devices with their start and end apart: 5 -> 0, of which waited for: 3 -> 0; matrix products, arithmetic and copies ran while one was open for 4% -> 0% of each run, Pallas kernels for 0% -> 0%
where the time goes in v1:
time: 161 us
  Pallas kernels  150 us (93%)
  local copies, waits for them, and re-layouts  10.6 us (7%)
    pallas_call x1, Pallas kernels, on_device(): pl.pallas_call(functools.partial(kernel, n, ndp, 256), out_shape=(wide, w...  150 us
    unnamed x17, local copies, waits for them, and re-layouts  10.6 us

profile of v1, /device:TPU:0, one launch (start us, length us, event | category | flops | bytes accessed | tf_op | source)
XLA Modules:
  0.0 161.0 jit_solution(4389541902091090642)
XLA Ops:
  0.6 1.4 copy.13.bi_ref
  2.0 149.7 %monarch.1 = (bf16[512,1536]{1,0:T(8,128)(2,1)}, bf16[512,1536]{1,0:T(8,128)(2,1)}, bf16[512,1536]{1,0:T(8,128)(2,1)}, bf16[512,1536]{1,0:T(8,128)(2,1)}, f32[4,64,128]{2,1,0:T(8,128)}, /*index=5*/f32[256,64]{1,0:T(8,128)}) custom-call(bf16[512,1536]{1,0:T(8,128)(2,1)} %bitcast.15, bf16[512,1536]{1,0:T(8,128)(2,1)} %bitcast.16, bf16[512,1536]{1,0:T(8,128)(2,1)} %bitcast.17, ...), custom_call_target="tpu_custom_call" | custom-call | flops 5637144576 | bytes 12582912 | tf_op jit(solution)/shard_map/monarch/pallas_call | solution.py:307
  151.8 0.0 copy-start.2
  151.8 2.8 %copy.20 = bf16[1,512,1536]{2,1,0:T(8,128)(2,1)} copy(bf16[1,512,1536]{2,1,0:T(8,128)(2,1)} %bitcast.13) | data formatting | bytes 3145728
  154.5 0.0 copy-done.2
  154.5 0.0 copy-start.1
  154.5 1.1 copy.21
  155.7 0.8 copy-done.1
  156.5 0.0 copy-start
  156.5 1.1 copy.22
  157.7 0.8 copy-done
  158.5 0.0 copy-start.4
  158.5 0.0 copy-start.3
  158.5 1.1 copy.23
  159.6 0.0 copy-done.4
  159.6 0.7 copy.24
  160.3 0.0 copy-done.3
  160.3 0.7 copy.25
Async XLA Ops:
  151.8 2.8 %copy-start.2 = (bf16[512,1536]{1,0:T(8,128)(2,1)S(1)}, bf16[512,1536]{1,0:T(8,128)(2,1)}, u32[]{:S(2)}) copy-start(bf16[512,1536]{1,0:T(8,128)(2,1)} %get-tuple-element.13) | copy-start | bytes 4718596
  154.5 2.0 %copy-start.1 = (bf16[512,1536]{1,0:T(8,128)(2,1)S(1)}, bf16[512,1536]{1,0:T(8,128)(2,1)}, u32[]{:S(2)}) copy-start(bf16[512,1536]{1,0:T(8,128)(2,1)} %get-tuple-element.14) | copy-start | bytes 4718596
  156.5 2.0 %copy-start = (bf16[512,1536]{1,0:T(8,128)(2,1)S(1)}, bf16[512,1536]{1,0:T(8,128)(2,1)}, u32[]{:S(2)}) copy-start(bf16[512,1536]{1,0:T(8,128)(2,1)} %get-tuple-element.15) | copy-start | bytes 4718596
  158.5 1.1 copy-start.4
  158.5 1.8 %copy-start.3 = (f32[256,64]{1,0:T(8,128)S(1)}, f32[256,64]{1,0:T(8,128)}, u32[]{:S(2)}) copy-start(f32[256,64]{1,0:T(8,128)} %get-tuple-element.17) | copy-start | bytes 196612

commit v2 on v1

v2 whole, which is shorter than its diff:
```python
import functools

import jax
import jax.numpy as jnp
from jax import lax
from jax.experimental import pallas as pl
from jax.experimental.pallas import tpu as pltpu
from jax.sharding import PartitionSpec as P

F32 = jnp.float32
BF16 = jnp.bfloat16
G, F, H, M = range(4)


def log2(x):
    return x.bit_length() - 1


def iota(shape, dim):
    return lax.broadcasted_iota(jnp.int32, shape, dim)


def onehot(cond):
    return jnp.where(cond, 1.0, 0.0).astype(BF16)


def dot(a, b):
    return jnp.dot(a, b, preferred_element_type=F32)


def dot_nt(a, b):
    return lax.dot_general(a, b, (((1,), (1,)), ((), ())), preferred_element_type=F32)


def dot_tn(a, b):
    return lax.dot_general(a, b, (((0,), (0,)), ((), ())), preferred_element_type=F32)


def thirds(x):
    hi = x.astype(BF16)
    rest = x - hi.astype(F32)
    mid = rest.astype(BF16)
    return hi, mid, (rest - mid.astype(F32)).astype(BF16)


def kernel(
    n, ndp, halves, tile,
    q_in, k_in, v_in, c_in, w_ref, mx_ref, bi_ref,
    o_ref, gq_ref, gk_ref, gv_ref, gb_ref, gm_ref,
    gs, gr, fs, fr, hs, hr, ms, mr,
    prod, gfn, bmat, btm, wfull, wg, mg, pr, gms, gmr, gbs, gbr,
    q_ref, k_ref, v_ref, c_ref,
    send, recv, dsend, drecv, lsem, isem,
):
    rows, width = q_ref.shape
    blocks, bs = w_ref.shape[0], w_ref.shape[2]
    nnz, nb = bi_ref.shape
    offs = bs // n
    chunk = blocks * offs
    own = nb // ndp
    part = own * offs
    a_loc = w_ref.shape[1]
    me = lax.axis_index("seq")
    core = lax.axis_index("dp")

    def peer(i):
        return lax.rem(me + 1 + lax.rem(n // 2 - 1 + 4 * i, n - 1), n)

    def mate(i):
        return lax.rem(core + 1 + i, ndp)

    half = width // halves

    def fetch(u, kind):
        src = (c_in, q_in, k_in, v_in)[kind]
        dst = (c_ref, q_ref, k_ref, v_ref)[kind]
        span = slice(u * half, (u + 1) * half)
        return pltpu.make_async_copy(src.at[:, span], dst.at[:, span], isem.at[u, kind])

    for kinds in ((0, 1), (2, 3)):
        for u in range(halves):
            for kind in kinds:
                fetch(u, kind).start()

    barrier = pltpu.get_barrier_semaphore()

    @pl.loop(0, n - 1)
    def _(i):
        pl.semaphore_signal(
            barrier, inc=1, device_id={"dp": core, "seq": lax.rem(me + 1 + i, n)},
            device_id_type=pl.DeviceIdType.MESH,
        )

    @pl.loop(0, ndp - 1)
    def _(i):
        pl.semaphore_signal(
            barrier, inc=1, device_id={"dp": mate(i), "seq": me},
            device_id_type=pl.DeviceIdType.MESH,
        )

    pl.semaphore_wait(barrier, n + ndp - 2)

    def across(kind, u, src, dst, to, slot):
        return pltpu.make_async_remote_copy(
            src_ref=src.at[u, to], dst_ref=dst.at[u, slot],
            send_sem=send.at[kind, u, to], recv_sem=recv.at[kind, u, slot],
            device_id={"dp": core, "seq": to}, device_id_type=pl.DeviceIdType.MESH,
        )

    pairs = ((gs, gr), (fs, fr), (hs, hr), (ms, mr))

    def exchange(kind, u):
        src, dst = pairs[kind]
        before = kind * halves + u - 2

        @pl.loop(0, n - 1)
        def _(i):
            if before >= 0:
                across(before // halves, before % halves, *pairs[before // halves], peer(i), me).wait_send()
            across(kind, u, src, dst, peer(i), me).start()

        pltpu.make_async_copy(src.at[u, me], dst.at[u, me], lsem.at[kind, u]).start()

    def arrived(kind, u):
        src, dst = pairs[kind]

        @pl.loop(0, n - 1)
        def _(i):
            across(kind, u, src, dst, me, peer(i)).wait_recv()

        pltpu.make_async_copy(src.at[u, me], dst.at[u, me], lsem.at[kind, u]).wait()

    def left(kind, u):
        @pl.loop(0, n - 1)
        def _(i):
            across(kind, u, *pairs[kind], peer(i), me).wait_send()

    def beside(kind, src, dst, to, slot):
        return pltpu.make_async_remote_copy(
            src_ref=src, dst_ref=dst.at[slot],
            send_sem=dsend.at[kind, to], recv_sem=drecv.at[kind, slot],
            device_id={"dp": to, "seq": me}, device_id_type=pl.DeviceIdType.MESH,
        )

    def columns(u, body):
        @pl.loop(0, half // tile)
        def _(t):
            start = pl.multiple_of(t * tile, tile)
            body(pl.ds(u * half + start, tile), pl.ds(start, tile))

    def place(shape, row_dim):
        r = iota(shape, row_dim)
        rem = r & (chunk - 1)
        return (rem >> log2(offs)) * bs + (r >> log2(chunk)) * offs + (rem & (offs - 1))

    def to_chunks(parts, dst, u, cols):
        if offs % 8 == 0:
            for p in range(n):
                span = slice(p * offs, (p + 1) * offs)
                dst[u, p, :, cols] = jnp.concatenate([x[span] for x in parts], axis=0).astype(BF16)
        else:
            order = onehot(place((rows, rows), 0) == iota((rows, rows), 1))
            whole = jnp.concatenate(parts, axis=0).astype(BF16)
            dst[u, :, :, cols] = dot(order, whole).astype(BF16).reshape(n, chunk, tile)

    def from_chunks(src, u, cols):
        if offs % 8 == 0:
            pieces = [src[u, p, :, cols].astype(F32) for p in range(n)]
            return [
                jnp.concatenate([x[b * offs : (b + 1) * offs] for x in pieces], axis=0)
                for b in range(blocks)
            ]
        order = onehot(place((rows, rows), 1) == iota((rows, rows), 0))
        whole = dot(order, src[u, :, :, cols].reshape(rows, tile))
        return [whole[b * bs : (b + 1) * bs] for b in range(blocks)]

    @pl.loop(0, ndp - 1)
    def _(i):
        beside(0, w_ref, wg, mate(i), core).start()
        beside(1, mx_ref, mg, mate(i), core).start()

    for u in range(halves):
        fetch(u, 0).wait()
        fetch(u, 1).wait()

        def gate(cols, at):
            parts = []
            for b in range(blocks):
                span = slice(b * bs, (b + 1) * bs)
                parts.append(c_ref[span, cols].astype(F32) * q_ref[span, cols].astype(F32))
            to_chunks(parts, gs, u, at)

        columns(u, gate)
        exchange(G, u)

    wg[core] = w_ref[...]
    mg[core] = mx_ref[...]

    @pl.loop(0, ndp - 1)
    def _(i):
        beside(0, w_ref, wg, core, mate(i)).wait_recv()
        beside(1, mx_ref, mg, core, mate(i)).wait_recv()

    for h in range(ndp):
        wfull[:, h * a_loc : (h + 1) * a_loc, :] = wg[h]

    for u in range(halves):
        fetch(u, 2).wait()
        fetch(u, 3).wait()

        def first(cols, at):
            parts = []
            for b in range(blocks):
                span = slice(b * bs, (b + 1) * bs)
                x = (k_ref[span, cols].astype(F32) * v_ref[span, cols].astype(F32)).astype(BF16)
                prod[span, cols] = x
                parts.append(dot(wfull[b], x))
            to_chunks(parts, fs, u, at)

        columns(u, first)

    named = jnp.zeros((nb, nb), F32)
    index = bi_ref[...]
    for t in range(nnz):
        named = jnp.where(index[t : t + 1, :] == iota((nb, nb), 0), 1.0, named)
    named = named.astype(BF16)
    spread = onehot((iota((nb, rows), 1) >> log2(offs)) == iota((nb, rows), 0))
    same = ((iota((part, rows), 0) ^ iota((part, rows), 1)) & (offs - 1)) == 0
    r, c = iota((part, part), 0), iota((part, part), 1)
    by_block = onehot((r & (offs - 1)) * own + (r >> log2(offs)) == c)
    by_offset = onehot((c & (offs - 1)) * own + (c >> log2(offs)) == r)
    for h in range(ndp):
        span = slice(h * part, (h + 1) * part)
        lift = onehot((iota((part, nb), 0) >> log2(offs)) + h * own == iota((part, nb), 1))
        pattern = dot_nt(lift, named)
        pr[h] = pattern
        masked = (dot(by_block, mg[h]) * pattern).astype(BF16)
        bmat[span, :] = jnp.where(same, dot(masked, spread), 0.0).astype(BF16)
    btm[...] = bmat[...].T

    for u in range(halves):
        exchange(F, u)

    def second(matrix, kind, u, back):
        src, dst = pairs[kind][1], pairs[back][0]
        arrived(kind, u)

        def body(cols, at):
            x = src[u, :, :, at].reshape(rows, tile)
            dst[u, :, :, at] = dot(matrix[...], x).astype(BF16).reshape(n, chunk, tile)

        columns(u, body)
        exchange(back, u)

    for u in range(halves):
        second(btm, G, u, H)
    for u in range(halves):
        second(bmat, F, u, M)

    step = part // chunk
    for h in range(ndp):
        span = slice(h * step, (h + 1) * step)
        terms = sum(
            dot_nt(gr[u, span].reshape(part, half), fr[u].reshape(rows, half))
            for u in range(halves)
        )
        terms = jnp.where(same, terms, 0.0)
        kept = sum(dot_nt(x, spread) for x in thirds(terms))
        gms[h] = kept * pr[h]

    @pl.loop(0, ndp - 1)
    def _(i):
        beside(2, gms.at[mate(i)], gmr, mate(i), core).start()

    for u in range(halves):
        arrived(H, u)

        def grad_inputs(cols, at):
            parts = from_chunks(hr, u, at)
            for b in range(blocks):
                span = slice(b * bs, (b + 1) * bs)
                x = parts[b].astype(BF16)
                gfn[span, cols] = x
                gp = dot_tn(wfull[b], x)
                gk_ref[span, cols] = (gp * v_ref[span, cols].astype(F32)).astype(BF16)
                gv_ref[span, cols] = (gp * k_ref[span, cols].astype(F32)).astype(BF16)

        columns(u, grad_inputs)

    for b in range(blocks):
        span = slice(b * bs, (b + 1) * bs)
        terms = dot_nt(gfn[span, :], prod[span, :])
        for h in range(ndp):
            gbs[h, b] = terms[h * a_loc : (h + 1) * a_loc]

    @pl.loop(0, ndp - 1)
    def _(i):
        beside(3, gbs.at[mate(i)], gbr, mate(i), core).start()

    gmr[core] = gms[core]
    gbr[core] = gbs[core]

    @pl.loop(0, ndp - 1)
    def _(i):
        beside(2, gms.at[mate(i)], gmr, core, mate(i)).wait_recv()
        beside(3, gbs.at[mate(i)], gbr, core, mate(i)).wait_recv()

    gb_ref[...] = sum(gbr[h] for h in range(ndp))
    total = sum(gmr[h] for h in range(ndp))
    gm_ref[...] = sum(dot(by_offset, x) for x in thirds(total))

    @pl.loop(0, ndp - 1)
    def _(i):
        beside(0, w_ref, wg, mate(i), core).wait_send()
        beside(1, mx_ref, mg, mate(i), core).wait_send()
        beside(2, gms.at[mate(i)], gmr, mate(i), core).wait_send()
        beside(3, gbs.at[mate(i)], gbr, mate(i), core).wait_send()

    for u in range(halves):
        arrived(M, u)

        def outputs(cols, at):
            parts = from_chunks(mr, u, at)
            for b in range(blocks):
                span = slice(b * bs, (b + 1) * bs)
                o_ref[span, cols] = (q_ref[span, cols].astype(F32) * parts[b]).astype(BF16)
                gq_ref[span, cols] = (c_ref[span, cols].astype(F32) * parts[b]).astype(BF16)

        columns(u, outputs)

    for last in range(4 * halves - 2, 4 * halves):
        left(last // halves, last % halves)


def write_out(*refs):
    count = len(refs) // 2
    sems = refs[-1]
    copies = [
        pltpu.make_async_copy(refs[i], refs[count + i], sems.at[i]) for i in range(count)
    ]
    for copy in copies:
        copy.start()
    for copy in copies:
        copy.wait()


def on_device(n, ndp, query, key, value, block_weights, mix_weights, block_index, cotangent):
    _, rows, width = query.shape
    nb = block_index.shape[0]
    blocks, a_loc, bs = block_weights.shape
    offs, own, _ = mix_weights.shape
    chunk, part = blocks * offs, own * offs
    vmem = pl.BlockSpec(memory_space=pltpu.VMEM)
    anywhere = pl.BlockSpec(memory_space=pl.ANY)
    halves = 2
    moved = pltpu.VMEM((halves, n, chunk, width // halves), BF16)
    shapes = [((rows, width), BF16)] * 4 + [((blocks, a_loc, bs), F32), ((offs * own, nb), F32)]
    dma = pltpu.SemaphoreType.DMA
    outs = pl.pallas_call(
        functools.partial(kernel, n, ndp, halves, 256),
        out_shape=tuple(pltpu.VMEM(*shape) for shape in shapes),
        in_specs=[anywhere] * 4 + [vmem] * 3,
        out_specs=(vmem,) * 6,
        scratch_shapes=[moved] * 8 + [
            pltpu.VMEM((rows, width), BF16),
            pltpu.VMEM((rows, width), BF16),
            pltpu.VMEM((rows, rows), BF16),
            pltpu.VMEM((rows, rows), BF16),
            pltpu.VMEM((blocks, bs, bs), BF16),
            pltpu.VMEM((ndp, blocks, a_loc, bs), BF16),
            pltpu.VMEM((ndp, offs * own, nb), BF16),
            pltpu.VMEM((ndp, part, nb), F32),
            pltpu.VMEM((ndp, part, nb), F32),
            pltpu.VMEM((ndp, part, nb), F32),
            pltpu.VMEM((ndp, blocks, a_loc, bs), F32),
            pltpu.VMEM((ndp, blocks, a_loc, bs), F32),
            *[pltpu.VMEM((rows, width), BF16)] * 4,
            dma((4, halves, n)), dma((4, halves, n)), dma((4, ndp)), dma((4, ndp)),
            dma((4, halves)), dma((halves, 4)),
        ],
        compiler_params=pltpu.CompilerParams(
            collective_id=0, has_side_effects=True, vmem_limit_bytes=48 * 1024 * 1024
        ),
        cost_estimate=pl.CostEstimate(
            flops=7 * 2 * rows * rows * width, bytes_accessed=16 * rows * width, transcendentals=0
        ),
        name="monarch",
    )(
        query[0], key[0], value[0], cotangent[0],
        block_weights, mix_weights.reshape(offs * own, nb), block_index.T,
    )
    outs = pl.pallas_call(
        write_out,
        out_shape=tuple(jax.ShapeDtypeStruct(*shape) for shape in shapes),
        in_specs=[vmem] * 6,
        out_specs=(anywhere,) * 6,
        scratch_shapes=[dma((6,))],
        name="write_out",
    )(*outs)
    output, grad_query, grad_key, grad_value, grad_blocks, grad_mix = outs
    return (
        output[None], grad_query[None], grad_key[None], grad_value[None],
        grad_blocks, grad_mix.reshape(offs, own, nb),
    )


def solution(mesh):
    wide, split = P("dp", "seq", None), P("seq", "dp", None)
    return jax.shard_map(
        functools.partial(on_device, mesh.shape["seq"], mesh.shape["dp"]),
        mesh=mesh,
        in_specs=(wide, wide, wide, split, split, P(), wide),
        out_specs=(wide, wide, wide, wide, split, split),
        check_vma=False,
    )
```

time: 161 us -> 159 us (0.988)
  local copies, waits for them, and re-layouts: 10.6 us -> 5.91 us
  Pallas kernels: 150 us -> 152 us
    unnamed x17 -> x12, local copies, waits for them, and re-layouts: 10.6 us -> 5.91 us
    pallas_call x1 -> x2, Pallas kernels: 150 us -> 152 us  [the longest x1 147 us: on_device(): pl.pallas_call(functools.partial(kernel, n, ndp, halves, 256), out_shape=...]
where the time goes in v2:
time: 159 us
  Pallas kernels  152 us (96%)
  local copies, waits for them, and re-layouts  5.91 us (4%)
    pallas_call x1, Pallas kernels, on_device(): pl.pallas_call(functools.partial(kernel, n, ndp, halves, 256), out_shape=...  147 us
    unnamed x12, local copies, waits for them, and re-layouts  5.91 us
    pallas_call x1, Pallas kernels, on_device(): pl.pallas_call(write_out, out_shape=tuple((jax.ShapeDtypeStruct(*shape) f...  5.61 us

profile of v2, /device:TPU:0, one launch (start us, length us, event | category | flops | bytes accessed | tf_op | source)
XLA Modules:
  0.0 159.0 jit_solution(9072426054347502764)
XLA Ops:
  0.6 146.8 %monarch.1 = (bf16[512,1536]{1,0:T(8,128)(2,1)S(1)}, bf16[512,1536]{1,0:T(8,128)(2,1)S(1)}, bf16[512,1536]{1,0:T(8,128)(2,1)S(1)}, bf16[512,1536]{1,0:T(8,128)(2...) custom-call(bf16[512,1536]{1,0:T(8,128)(2,1)} %bitcast.11, bf16[512,1536]{1,0:T(8,128)(2,1)} %bitcast.12, ...), custom_call_target="tpu_custom_call" | custom-call | flops 5637144576 | bytes 12582912 | tf_op jit(solution)/shard_map/monarch/pallas_call | solution.py:359
  147.5 0.0 copy-start
  147.5 1.1 copy-done
  148.6 0.0 copy-start.1
  148.6 1.2 copy-done.1
  149.8 0.0 copy-start.2
  149.8 1.1 copy-done.2
  150.9 0.0 copy-start.3
  150.9 1.2 copy-done.3
  152.1 0.0 copy-start.4
  152.1 0.6 copy-done.4
  152.7 0.0 copy-start.5
  152.7 0.6 copy-done.5
  153.4 5.6 %write_out.1 = (bf16[512,1536]{1,0:T(8,128)(2,1)}, bf16[512,1536]{1,0:T(8,128)(2,1)}, bf16[512,1536]{1,0:T(8,128)(2,1)}, bf16[512,1536]{1,0:T(8,128)(2,1)}, f32[4,64,128]{2,1,0:T(8,128)}, /*index=5*/f32[256,64]{1,0:T(8,128)}) custom-call(bf16[512,1536]{1,0:T(8,128)(2,1)} %copy-done, bf16[512,1536]{1,0:T(8,128)(2,1)} %copy-done.1, ...), custom_call_target="tpu_custom_call" | custom-call | tf_op jit(solution)/shard_map/write_out/pallas_call | solution.py:392
Async XLA Ops:
  147.5 1.1 copy-start
  148.6 1.2 copy-start.1
  149.8 1.1 copy-start.2
  150.9 1.2 copy-start.3
  152.1 0.7 copy-start.4
  152.7 0.6 copy-start.5

commit v3 on v2

--- a/solution.py
+++ b/solution.py
@@ -44,7 +44,7 @@
 
 
 def kernel(
-    n, ndp, halves, tile,
+    n, ndp, cuts, tile,
     q_in, k_in, v_in, c_in, w_ref, mx_ref, bi_ref,
     o_ref, gq_ref, gk_ref, gv_ref, gb_ref, gm_ref,
     gs, gr, fs, fr, hs, hr, ms, mr,
@@ -69,16 +69,17 @@
     def mate(i):
         return lax.rem(core + 1 + i, ndp)
 
-    half = width // halves
+    piece = width // cuts
+    depth = cuts
 
     def fetch(u, kind):
         src = (c_in, q_in, k_in, v_in)[kind]
         dst = (c_ref, q_ref, k_ref, v_ref)[kind]
-        span = slice(u * half, (u + 1) * half)
+        span = slice(u * piece, (u + 1) * piece)
         return pltpu.make_async_copy(src.at[:, span], dst.at[:, span], isem.at[u, kind])
 
     for kinds in ((0, 1), (2, 3)):
-        for u in range(halves):
+        for u in range(cuts):
             for kind in kinds:
                 fetch(u, kind).start()
 
@@ -97,8 +98,6 @@
             barrier, inc=1, device_id={"dp": mate(i), "seq": me},
             device_id_type=pl.DeviceIdType.MESH,
         )
-
-    pl.semaphore_wait(barrier, n + ndp - 2)
 
     def across(kind, u, src, dst, to, slot):
         return pltpu.make_async_remote_copy(
@@ -111,12 +110,12 @@
 
     def exchange(kind, u):
         src, dst = pairs[kind]
-        before = kind * halves + u - 2
+        before = kind * cuts + u - depth
 
         @pl.loop(0, n - 1)
         def _(i):
             if before >= 0:
-                across(before // halves, before % halves, *pairs[before // halves], peer(i), me).wait_send()
+                across(before // cuts, before % cuts, *pairs[before // cuts], peer(i), me).wait_send()
             across(kind, u, src, dst, peer(i), me).start()
 
         pltpu.make_async_copy(src.at[u, me], dst.at[u, me], lsem.at[kind, u]).start()
@@ -143,10 +142,10 @@
         )
 
     def columns(u, body):
-        @pl.loop(0, half // tile)
+        @pl.loop(0, piece // tile)
         def _(t):
             start = pl.multiple_of(t * tile, tile)
-            body(pl.ds(u * half + start, tile), pl.ds(start, tile))
+            body(pl.ds(u * piece + start, tile), pl.ds(start, tile))
 
     def place(shape, row_dim):
         r = iota(shape, row_dim)
@@ -174,12 +173,7 @@
         whole = dot(order, src[u, :, :, cols].reshape(rows, tile))
         return [whole[b * bs : (b + 1) * bs] for b in range(blocks)]
 
-    @pl.loop(0, ndp - 1)
-    def _(i):
-        beside(0, w_ref, wg, mate(i), core).start()
-        beside(1, mx_ref, mg, mate(i), core).start()
-
-    for u in range(halves):
+    for u in range(cuts):
         fetch(u, 0).wait()
         fetch(u, 1).wait()
 
@@ -191,7 +185,14 @@
             to_chunks(parts, gs, u, at)
 
         columns(u, gate)
+        if u == 0:
+            pl.semaphore_wait(barrier, n + ndp - 2)
         exchange(G, u)
+
+    @pl.loop(0, ndp - 1)
+    def _(i):
+        beside(0, w_ref, wg, mate(i), core).start()
+        beside(1, mx_ref, mg, mate(i), core).start()
 
     wg[core] = w_ref[...]
     mg[core] = mx_ref[...]
@@ -204,7 +205,7 @@
     for h in range(ndp):
         wfull[:, h * a_loc : (h + 1) * a_loc, :] = wg[h]
 
-    for u in range(halves):
+    for u in range(cuts):
         fetch(u, 2).wait()
         fetch(u, 3).wait()
 
@@ -238,7 +239,7 @@
         bmat[span, :] = jnp.where(same, dot(masked, spread), 0.0).astype(BF16)
     btm[...] = bmat[...].T
 
-    for u in range(halves):
+    for u in range(cuts):
         exchange(F, u)
 
     def second(matrix, kind, u, back):
@@ -252,17 +253,17 @@
         columns(u, body)
         exchange(back, u)
 
-    for u in range(halves):
+    for u in range(cuts):
         second(btm, G, u, H)
-    for u in range(halves):
+    for u in range(cuts):
         second(bmat, F, u, M)
 
     step = part // chunk
     for h in range(ndp):
         span = slice(h * step, (h + 1) * step)
         terms = sum(
-            dot_nt(gr[u, span].reshape(part, half), fr[u].reshape(rows, half))
-            for u in range(halves)
+            dot_nt(gr[u, span].reshape(part, piece), fr[u].reshape(rows, piece))
+            for u in range(cuts)
         )
         terms = jnp.where(same, terms, 0.0)
         kept = sum(dot_nt(x, spread) for x in thirds(terms))
@@ -272,7 +273,7 @@
     def _(i):
         beside(2, gms.at[mate(i)], gmr, mate(i), core).start()
 
-    for u in range(halves):
+    for u in range(cuts):
         arrived(H, u)
 
         def grad_inputs(cols, at):
@@ -316,7 +317,7 @@
         beside(2, gms.at[mate(i)], gmr, mate(i), core).wait_send()
         beside(3, gbs.at[mate(i)], gbr, mate(i), core).wait_send()
 
-    for u in range(halves):
+    for u in range(cuts):
         arrived(M, u)
 
         def outputs(cols, at):
@@ -328,8 +329,8 @@
 
         columns(u, outputs)
 
-    for last in range(4 * halves - 2, 4 * halves):
-        left(last // halves, last % halves)
+    for last in range(4 * cuts - depth, 4 * cuts):
+        left(last // cuts, last % cuts)
 
 
 def write_out(*refs):
@@ -352,12 +353,12 @@
     chunk, part = blocks * offs, own * offs
     vmem = pl.BlockSpec(memory_space=pltpu.VMEM)
     anywhere = pl.BlockSpec(memory_space=pl.ANY)
-    halves = 2
-    moved = pltpu.VMEM((halves, n, chunk, width // halves), BF16)
+    cuts = 3
+    moved = pltpu.VMEM((cuts, n, chunk, width // cuts), BF16)
     shapes = [((rows, width), BF16)] * 4 + [((blocks, a_loc, bs), F32), ((offs * own, nb), F32)]
     dma = pltpu.SemaphoreType.DMA
     outs = pl.pallas_call(
-        functools.partial(kernel, n, ndp, halves, 256),
+        functools.partial(kernel, n, ndp, cuts, 256),
         out_shape=tuple(pltpu.VMEM(*shape) for shape in shapes),
         in_specs=[anywhere] * 4 + [vmem] * 3,
         out_specs=(vmem,) * 6,
@@ -375,8 +376,8 @@
             pltpu.VMEM((ndp, blocks, a_loc, bs), F32),
             pltpu.VMEM((ndp, blocks, a_loc, bs), F32),
             *[pltpu.VMEM((rows, width), BF16)] * 4,
-            dma((4, halves, n)), dma((4, halves, n)), dma((4, ndp)), dma((4, ndp)),
-            dma((4, halves)), dma((halves, 4)),
+            dma((4, cuts, n)), dma((4, cuts, n)), dma((4, ndp)), dma((4, ndp)),
+            dma((4, cuts)), dma((cuts, 4)),
         ],
         compiler_params=pltpu.CompilerParams(
             collective_id=0, has_side_effects=True, vmem_limit_bytes=48 * 1024 * 1024
@@ -395,6 +396,7 @@
         in_specs=[vmem] * 6,
         out_specs=(anywhere,) * 6,
         scratch_shapes=[dma((6,))],
+        compiler_params=pltpu.CompilerParams(vmem_limit_bytes=8 * 1024 * 1024),
         name="write_out",
     )(*outs)
     output, grad_query, grad_key, grad_value, grad_blocks, grad_mix = outs

time: 159 us -> 152 us (0.956)
  local copies, waits for them, and re-layouts: 5.91 us -> 0 us
    unnamed x12 -> x0, local copies, waits for them, and re-layouts: 5.91 us -> none
    pallas_call x1, Pallas kernels: 5.61 us -> 2.78 us  [on_device(): pl.pallas_call(write_out, out_shape=tuple((jax.ShapeDtypeStruct(*shape) f...]
where the time goes in v3:
time: 152 us
  Pallas kernels  151 us (99%)
    pallas_call x1, Pallas kernels, on_device(): pl.pallas_call(functools.partial(kernel, n, ndp, cuts, 256), out_shape=tu...  148 us

profile of v3, /device:TPU:0, one launch (start us, length us, event | category | flops | bytes accessed | tf_op | source)
XLA Modules:
  0.0 151.7 jit_solution(12088161181986003897)
XLA Ops:
  0.6 148.2 %monarch.1 = (bf16[512,1536]{1,0:T(8,128)(2,1)S(1)}, bf16[512,1536]{1,0:T(8,128)(2,1)S(1)}, bf16[512,1536]{1,0:T(8,128)(2,1)S(1)}, bf16[512,1536]{1,0:T(8,128)(2...) custom-call(bf16[512,1536]{1,0:T(8,128)(2,1)} %bitcast.11, bf16[512,1536]{1,0:T(8,128)(2,1)} %bitcast.12, ...), custom_call_target="tpu_custom_call" | custom-call | flops 5637144576 | bytes 12582912 | tf_op jit(solution)/shard_map/monarch/pallas_call | solution.py:360
  148.9 2.8 %write_out.1 = (bf16[512,1536]{1,0:T(8,128)(2,1)}, bf16[512,1536]{1,0:T(8,128)(2,1)}, bf16[512,1536]{1,0:T(8,128)(2,1)}, bf16[512,1536]{1,0:T(8,128)(2,1)}, f32[4,64,128]{2,1,0:T(8,128)}, /*index=5*/f32[256,64]{1,0:T(8,128)}) custom-call(bf16[512,1536]{1,0:T(8,128)(2,1)S(1)} %get-tuple-element.18.refs_0_, bf16[512,1536]{1,0:T(8,128)(2,1)S(1)} %get-tuple-element.19.refs_1_, ...), custom_call_target="tpu_custom_call" | custom-call | tf_op jit(solution)/shard_map/write_out/pallas_call | solution.py:393

commit v4 on v3

--- a/solution.py
+++ b/solution.py
@@ -64,7 +64,7 @@
     core = lax.axis_index("dp")
 
     def peer(i):
-        return lax.rem(me + 1 + lax.rem(n // 2 - 1 + 4 * i, n - 1), n)
+        return lax.rem(me + 1 + lax.rem(n // 2 - 1 + 4 * (i + 2 * core), n - 1), n)
 
     def mate(i):
         return lax.rem(core + 1 + i, ndp)
@@ -353,7 +353,7 @@
     chunk, part = blocks * offs, own * offs
     vmem = pl.BlockSpec(memory_space=pltpu.VMEM)
     anywhere = pl.BlockSpec(memory_space=pl.ANY)
-    cuts = 3
+    cuts = 2
     moved = pltpu.VMEM((cuts, n, chunk, width // cuts), BF16)
     shapes = [((rows, width), BF16)] * 4 + [((blocks, a_loc, bs), F32), ((offs * own, nb), F32)]
     dma = pltpu.SemaphoreType.DMA

time: 152 us -> 150 us (0.987)
  Pallas kernels: 151 us -> 149 us
    pallas_call x1, Pallas kernels: 148 us -> 147 us  [on_device(): pl.pallas_call(functools.partial(kernel, n, ndp, cuts, 256), out_shape=tu...]
where the time goes in v4:
time: 150 us
  Pallas kernels  149 us (99%)
    pallas_call x1, Pallas kernels, on_device(): pl.pallas_call(functools.partial(kernel, n, ndp, cuts, 256), out_shape=tu...  147 us

profile of v4, /device:TPU:0, one launch (start us, length us, event | category | flops | bytes accessed | tf_op | source)
XLA Modules:
  0.0 150.0 jit_solution(14129389648998243842)
XLA Ops:
  0.6 146.5 %monarch.1 = (bf16[512,1536]{1,0:T(8,128)(2,1)S(1)}, bf16[512,1536]{1,0:T(8,128)(2,1)S(1)}, bf16[512,1536]{1,0:T(8,128)(2,1)S(1)}, bf16[512,1536]{1,0:T(8,128)(2...) custom-call(bf16[512,1536]{1,0:T(8,128)(2,1)} %bitcast.11, bf16[512,1536]{1,0:T(8,128)(2,1)} %bitcast.12, ...), custom_call_target="tpu_custom_call" | custom-call | flops 5637144576 | bytes 12582912 | tf_op jit(solution)/shard_map/monarch/pallas_call | solution.py:360
  147.2 2.8 %write_out.1 = (bf16[512,1536]{1,0:T(8,128)(2,1)}, bf16[512,1536]{1,0:T(8,128)(2,1)}, bf16[512,1536]{1,0:T(8,128)(2,1)}, bf16[512,1536]{1,0:T(8,128)(2,1)}, f32[4,64,128]{2,1,0:T(8,128)}, /*index=5*/f32[256,64]{1,0:T(8,128)}) custom-call(bf16[512,1536]{1,0:T(8,128)(2,1)S(1)} %get-tuple-element.18.refs_0_, bf16[512,1536]{1,0:T(8,128)(2,1)S(1)} %get-tuple-element.19.refs_1_, ...), custom_call_target="tpu_custom_call" | custom-call | tf_op jit(solution)/shard_map/write_out/pallas_call | solution.py:393
